TPU v7x, 32 devices: a whole 2x2x4 slice. The times are simulated.
32 devices in a mesh: group: 2 (over x), src: 4 (over z), tile: 4 (over y, core).
Axes of the slice: x: 2, y: 2, z: 4, core: 2. Of those that a mesh axis runs over, the one named last changes fastest.
Arguments:
- mask_param: float32 [2048, 256], P(('group', 'tile')), parts along dimension 0, may hold values from -6 to 6
- target_image: float32 [2048, 256], P(('group', 'tile')), parts along dimension 0, may hold values from 0 to 1
- source_weights: float32 [128], P(('group', 'src')), parts along dimension 0, may hold values from 0.36 to 8.2
- source_shifts: int32 [64, 2], P('src'), may hold values from -16 to 16, as said below
- pupil_map: float32 [2, 32, 32], replicated, may hold values from -1.4 to 1.4, as said below
Outputs:
- mask_final: float32 [2048, 256], P(('group', 'tile')), parts along dimension 0
- weights_final: float32 [128], P(('group', 'src')), parts along dimension 0
There are 2 independent parts, one for each index of `group`. A program takes and returns all parts, laid end to end along the dimension named above; an argument that names none is the same for every part. Nothing has to cross between parts.
Inputs may be any that keep to these rules, and one draw needn't show every extreme that they name: `source_shifts`: each of the two columns takes the value 16 on some source and the value -16 on another. `pupil_map`: zero outside the disc of radius 32 // 2 - 1 around box index (16, 16).
All inputs are finite; a program needn't handle non-finite values.
Results may differ from a plain program's by a relative error of at most 0.0003.
Values sent between devices are 32-bit elements; how exact they have to be, the bound alone decides.
A program may use at most 64 MiB of HBM per device.

v0:
```python
import functools
import math

import jax
import jax.numpy as jnp
import numpy as np
from jax import lax
from jax.experimental import pallas as pl
from jax.experimental.pallas import tpu as pltpu
from jax.sharding import PartitionSpec as P

MARGIN = 64
MAX_SHIFT = 16
INNER_STEPS = 2
MESH = pl.DeviceIdType.MESH
mask_rate = 0.5
weight_rate = 0.3
tiny_eps = 1e-06
f32 = jnp.float32
bf16 = jnp.bfloat16


def angle(freqs, pixels, period):
    return np.mod(np.outer(freqs, pixels), period) * (2.0 * math.pi / period)


def dirichlet(pixels, period, box):
    grid = 2 * box
    diffs = np.arange(-(box - 1), box)
    left = angle(pixels, diffs, period)
    right = angle(diffs, np.arange(grid), grid)
    return (np.cos(left) @ np.cos(right) + np.sin(left) @ np.sin(right)) / grid


def tables(period, tile, box):
    grid = 2 * box
    wide = np.arange(grid) - box
    row = angle(wide, np.arange(period), period)
    col = angle(wide, np.arange(tile), period)
    g = angle(np.arange(grid), np.arange(grid), grid)
    c, s = np.cos(g), np.sin(g)
    k1 = dirichlet(np.arange(tile) + MARGIN, period, box)
    k2 = dirichlet(np.arange(tile), period, box)
    k2d = np.concatenate([k2.T, k2.T], 0)
    return dict(
        rf=np.concatenate([np.cos(row), np.sin(row)], 0),
        cf=np.concatenate([np.cos(col), np.sin(col)], 0).T,
        c2=np.block([[c, s], [-s, c]]),
        c2t=np.block([[c, -s], [s, c]]),
        cs=np.concatenate([c, s], 0),
        k1=k1,
        k1t=k1.T,
        k2d=k2d,
        k2dt=k2d.T,
        col=np.block([[np.cos(col), np.sin(col)], [-np.sin(col), np.cos(col)]]),
        rfa=np.concatenate([np.cos(row), -np.sin(row)], 0).T,
    )


NAMES = ("rf", "cf", "c2", "c2t", "cs", "k1", "k1t", "k2d", "k2dt", "col", "rfa")


def split_np(value):
    value = value.astype(np.float32)
    high = value.astype(jnp.bfloat16)
    low = (value - high.astype(np.float32)).astype(jnp.bfloat16)
    return high, low


def split(value):
    high = value.astype(bf16)
    return high, (value - high.astype(f32)).astype(bf16)


def dot(a, b):
    return jnp.dot(a, b, preferred_element_type=f32)


def dot3(a, b):
    return dot(a[0], b[0]) + (dot(a[0], b[1]) + dot(a[1], b[0]))


def kernel(ns, nt, scale, *refs):
    mask_ref, target_ref, wl_ref, wb_ref, pa_ref, pb_ref = refs[:6]
    consts = {
        name: (refs[6 + 2 * i], refs[7 + 2 * i]) for i, name in enumerate(NAMES)
    }
    refs = refs[6 + 2 * len(NAMES):]
    mask_out, weights_out = refs[:2]
    (params, grid, halo, dose_buf, power_buf, back_buf, next_buf, sq_buf, sg_buf, ss_buf,
     src_send, src_recv, tile_send, tile_recv) = refs[2:]
    group = lax.axis_index("group")
    src = lax.axis_index("src")
    tile = lax.axis_index("tile")
    size = mask_ref.shape[1]
    period = size + 2 * MARGIN
    count = wb_ref.shape[0]
    width = pa_ref.shape[1]
    half = width // 2

    def table(name):
        return consts[name][0][...], consts[name][1][...]

    def src_peer(r):
        return (group, lax.rem(src + r, ns), tile)

    def tile_peer(r):
        return (group, src, lax.rem(tile + r, nt))

    pending = []
    used = dict(src=0, tile=0)

    def start(axis, source, target, peer):
        at = used[axis]
        used[axis] = at + 1
        sends, recvs = (src_send, src_recv) if axis == "src" else (tile_send, tile_recv)
        copy = pltpu.make_async_remote_copy(
            src_ref=source, dst_ref=target, send_sem=sends.at[at], recv_sem=recvs.at[at],
            device_id=peer, device_id_type=MESH,
        )
        copy.start()
        pending.append(copy)
        return copy

    def spread_src(buf):
        return [start("src", buf.at[src], buf.at[src], src_peer(r)) for r in range(1, ns)]

    def spread_tile(buf):
        return [start("tile", buf.at[tile], buf.at[tile], tile_peer(r)) for r in range(1, nt)]

    def landed(copies):
        for copy in copies:
            copy.wait_recv()

    def total(buf, peers):
        value = buf[0]
        for i in range(1, peers):
            value = value + buf[i]
        return value

    barrier = pltpu.get_barrier_semaphore()
    for r in range(1, ns):
        pl.semaphore_signal(barrier, inc=1, device_id=src_peer(r), device_id_type=MESH)
    for r in range(1, nt):
        pl.semaphore_signal(barrier, inc=1, device_id=tile_peer(r), device_id_type=MESH)
    pl.semaphore_wait(barrier, ns + nt - 2)

    up = start("tile", mask_ref.at[pl.ds(size - MARGIN, MARGIN)], halo.at[0], tile_peer(1))
    down = start("tile", mask_ref.at[pl.ds(0, MARGIN)], halo.at[1], tile_peer(nt - 1))
    dose_buf[src] = wl_ref[...]
    dose_copies = spread_src(dose_buf)
    params[pl.ds(MARGIN, size)] = mask_ref[...]
    landed([up, down])
    params[pl.ds(0, MARGIN)] = halo[0]
    params[pl.ds(MARGIN + size, MARGIN)] = halo[1]
    landed(dose_copies)
    dose = jnp.sum(total(dose_buf, ns)[0:1], axis=1, keepdims=True)
    inv_dose = 1.0 / dose

    has_prev = (tile > 0).astype(f32)
    has_next = (tile < nt - 1).astype(f32)
    row_id = lax.broadcasted_iota(jnp.int32, (period, size), 0)
    keep = jnp.where(row_id < MARGIN, has_prev, jnp.where(row_id >= MARGIN + size, has_next, 1.0))
    lane = lax.broadcasted_iota(jnp.int32, (half, width), 1)
    sign = jnp.where(lane < half, 1.0, -1.0).astype(f32)

    def swap(value):
        return pltpu.roll(value, half, 1)

    def sigmoid_mask():
        return keep / (1.0 + jnp.exp(-params[...]))

    def imaging(mask, step):
        first = dot3(table("rf"), split(mask))
        quad = dot3(split(first), table("cf")) * scale
        spec = sign * quad[:half] - swap(quad[half:])
        spec_swap = swap(spec)
        parts = []
        for s in range(count):
            rows = pl.ds(s * half, half)
            parts.append(pa_ref[rows] * spec + pb_ref[rows] * spec_swap)
        lit = jnp.concatenate(parts, 0)
        mid = dot3(split(lit), table("c2"))
        cs = table("cs")
        power = jnp.zeros((half, width), f32)
        for s in range(count):
            both = dot3(cs, split(mid[s * half:(s + 1) * half]))
            z = both[:half] - sign * swap(both[half:])
            grid[s] = z
            power = power + wb_ref[s:s + 1] * (z * z)
        buf = power_buf.at[step]
        buf[src] = power
        landed(spread_src(buf))
        power = total(buf, ns)
        bright = dot3(split(dot3(table("k1"), split(power))), table("k2d")) * inv_dose
        misfit = bright - target_ref[...]
        pull = dot3(split(dot3(table("k1t"), split(misfit))), table("k2dt"))
        return bright, misfit, pull

    for step in range(INNER_STEPS):
        mask = sigmoid_mask()
        bright, misfit, pull = imaging(mask, step)
        cs = table("cs")
        parts = []
        for s in range(count):
            both = dot3(cs, split(pull * grid[s]))
            parts.append(both[:half] + sign * swap(both[half:]))
        box = dot3(split(jnp.concatenate(parts, 0)), table("c2t"))
        one = jnp.zeros((half, width), f32)
        two = jnp.zeros((half, width), f32)
        for s in range(count):
            rows = pl.ds(s * half, half)
            value = wb_ref[s:s + 1] * box[s * half:(s + 1) * half]
            one = one + pa_ref[rows] * value
            two = two + pb_ref[rows] * value
        buf = back_buf.at[step]
        buf[src] = (one + swap(two)) * (2.0 * scale * inv_dose)
        landed(spread_src(buf))
        own = next_buf.at[step]
        back = total(buf, ns)
        own[2] = back
        to_next = start("tile", own.at[2], own.at[0], tile_peer(1))
        to_prev = start("tile", own.at[2], own.at[1], tile_peer(nt - 1))
        col = table("col")

        def values(spectrum):
            wide = dot3(split(spectrum), col)
            return split(jnp.concatenate([wide[:, :size], wide[:, size:]], 0))

        grad = dot3(table("rfa"), values(back))
        landed([to_next, to_prev])
        rim = 2 * MARGIN
        high, low = consts["rfa"]
        tail = pl.ds(period - rim, rim)
        before = dot3((high[tail], low[tail]), values(own[0] * has_prev))
        after = dot3((high[0:rim], low[0:rim]), values(own[1] * has_next))
        grad = jnp.concatenate(
            [grad[:rim] + before, grad[rim:period - rim], grad[period - rim:] + after], 0
        )
        grad = grad * (mask * (1.0 - mask))
        core = grad[MARGIN:MARGIN + size]
        square = jnp.sum(core * core, axis=0, keepdims=True)
        square = jnp.sum(square, axis=1, keepdims=True)
        buf = sq_buf.at[step]
        buf[tile] = jnp.broadcast_to(square, sq_buf.shape[2:])
        landed(spread_tile(buf))
        square = total(buf, nt)[0:1, 0:1]
        rms = jnp.sqrt(square / float(nt * size * size) + tiny_eps)
        params[...] = params[...] - grad * (mask_rate / rms)
    mask_out[...] = params[pl.ds(MARGIN, size)]

    bright, misfit, pull = imaging(sigmoid_mask(), INNER_STEPS)
    level = jnp.sum(misfit * bright, axis=0, keepdims=True)
    level = jnp.sum(level, axis=1, keepdims=True)
    rows = []
    for s in range(count):
        rows.append(jnp.sum(pull * (grid[s] * grid[s]), axis=0, keepdims=True))
    sums = jnp.sum(jnp.concatenate(rows, 0), axis=1, keepdims=True)
    sums = (sums - level) * inv_dose
    lanes = lax.broadcasted_iota(jnp.int32, (count, 128), 1)
    ids = lax.broadcasted_iota(jnp.int32, (count, 128), 0)
    packed = jnp.sum(jnp.where(lanes == ids, sums, 0.0), axis=0, keepdims=True)
    sg_buf[tile] = jnp.broadcast_to(packed, (8, 128))
    landed(spread_tile(sg_buf))
    slope = total(sg_buf, nt)
    ss_buf[src] = slope * slope
    landed(spread_src(ss_buf))
    square = jnp.sum(total(ss_buf, ns)[0:1], axis=1, keepdims=True)
    spread = jnp.sqrt(square / float(count * ns) + tiny_eps)
    weights_out[...] = wl_ref[...] * jnp.exp(-weight_rate * slope / spread)
    for copy in pending:
        copy.wait_send()


def per_device(ns, nt, mask_param, target_image, source_weights, source_shifts, pupil_map):
    size = mask_param.shape[1]
    box = pupil_map.shape[1]
    half = 2 * box
    width = 2 * half
    count = source_weights.shape[0]
    period = size + 2 * MARGIN
    consts = []
    made = tables(period, size, box)
    for name in NAMES:
        high, low = split_np(made[name])
        consts += [jnp.asarray(high), jnp.asarray(low)]
    highest = lax.Precision.HIGHEST
    base = jnp.arange(box, dtype=jnp.int32)[None, :, None] + MAX_SHIFT
    columns = jnp.arange(half, dtype=jnp.int32)[None, None, :]
    sel_rows = (base + source_shifts[:, 0, None, None] == columns).astype(f32)
    sel_cols = (base + source_shifts[:, 1, None, None] == columns).astype(f32)
    moved = jnp.einsum("cim,sij->scjm", pupil_map, sel_rows, precision=highest)
    moved = jnp.einsum("scjm,sml->scjl", moved, sel_cols, precision=highest)
    re, im = moved[:, 0], moved[:, 1]
    pa = jnp.concatenate([re, re], -1).reshape(count * half, width)
    pb = jnp.concatenate([-im, im], -1).reshape(count * half, width)
    wl = jnp.broadcast_to(jnp.pad(source_weights, (0, 128 - count))[None], (8, 128))
    wb = jnp.broadcast_to(source_weights[:, None], (count, width))
    vmem = pl.BlockSpec(memory_space=pltpu.VMEM)
    src_sends = (ns - 1) * (2 + 2 * INNER_STEPS + 1)
    tile_sends = 2 + INNER_STEPS * (2 + nt - 1) + (nt - 1)
    args = (mask_param, target_image, wl, wb, pa, pb, *consts)
    mask_final, weights_final = pl.pallas_call(
        functools.partial(kernel, ns, nt, 1.0 / (period * size)),
        out_shape=(
            jax.ShapeDtypeStruct(mask_param.shape, f32),
            jax.ShapeDtypeStruct((8, 128), f32),
        ),
        in_specs=[vmem] * len(args),
        out_specs=(vmem, vmem),
        scratch_shapes=[
            pltpu.VMEM((period, size), f32),
            pltpu.VMEM((count, half, width), f32),
            pltpu.VMEM((2, MARGIN, size), f32),
            pltpu.VMEM((ns, 8, 128), f32),
            pltpu.VMEM((INNER_STEPS + 1, ns, half, width), f32),
            pltpu.VMEM((INNER_STEPS, ns, half, width), f32),
            pltpu.VMEM((INNER_STEPS, 3, half, width), f32),
            pltpu.VMEM((INNER_STEPS, nt, 8, 128), f32),
            pltpu.VMEM((nt, 8, 128), f32),
            pltpu.VMEM((ns, 8, 128), f32),
            pltpu.SemaphoreType.DMA((src_sends,)),
            pltpu.SemaphoreType.DMA((src_sends,)),
            pltpu.SemaphoreType.DMA((tile_sends,)),
            pltpu.SemaphoreType.DMA((tile_sends,)),
        ],
        compiler_params=pltpu.CompilerParams(
            collective_id=0, has_side_effects=True, vmem_limit_bytes=48 * 1024 * 1024
        ),
    )(*args)
    return mask_final, weights_final[0, :count]


def solution(mesh):
    in_specs = (
        P(("group", "tile"), None),
        P(("group", "tile"), None),
        P(("group", "src")),
        P("src", None),
        P(),
    )
    out_specs = (P(("group", "tile"), None), P(("group", "src")))
    return jax.shard_map(
        functools.partial(per_device, mesh.shape["src"], mesh.shape["tile"]),
        mesh=mesh, in_specs=in_specs, out_specs=out_specs, check_vma=False,
    )
```

profile of v0, /device:TPU:0, one launch (start us, length us, event | category | flops | bytes accessed | tf_op | source)
XLA Modules:
  0.0 65.7 jit_solution(1272871820258822951)
XLA Ops:
  0.6 0.0 copy-start
  0.6 0.8 %slice_bitcast_fusion.1 = (s32[16]{0:T(128)S(1)}, s32[16]{0:T(128)S(1)}) fusion(s32[16,2]{0,1:T(2,128)} %param.30), kind=kLoop, calls=%fused_computation.14 | loop fusion | bytes 256 | tf_op jit(solution)/shard_map/slice | solution.py:291
  1.4 0.1 broadcast_add_fusion
  1.5 0.0 copy-done
  1.5 0.5 convolution_bitcast_fusion
  1.9 1.1 %fusion.3 = f32[16,2,64,64]{3,2,1,0:T(8,128)S(1)} fusion(f32[16,2,64,32]{2,3,1,0:T(8,128)S(1)} %convolution_bitcast_fusion, s32[16,32]{1,0:T(8,128)S(1)} %get-tuple-element.10), kind=kOutput, calls=%fused_computation.7 | convolution fusion | flops 50364416 | bytes 788480 | tf_op jit(solution)/shard_map/scjm,sml->scjl/dot_general | solution.py:293
  3.1 0.1 fusion.8
  3.2 0.0 copy-start.1
  3.2 0.0 copy-start.2
  3.2 0.0 copy-start.3
  3.2 0.0 copy-start.4
  3.3 0.0 copy-start.5
  3.3 0.0 copy-start.6
  3.3 0.0 copy-start.7
  3.3 0.0 copy-start.8
  3.3 0.0 copy-start.9
  3.3 0.0 copy-start.10
  3.3 0.0 copy-start.11
  3.3 0.0 copy-start.12
  3.4 0.0 copy-start.13
  3.4 0.0 copy-start.14
  3.4 0.0 copy-start.15
  3.4 0.0 copy-start.16
  3.4 0.0 copy-start.17
  3.4 0.0 copy-start.18
  3.4 0.0 copy-start.19
  3.4 0.0 copy-start.20
  3.5 0.0 copy-start.21
  3.5 0.0 copy-start.22
  3.5 0.0 copy-start.23
  3.5 0.0 copy-start.24
  3.5 0.3 pad_maximum_fusion
  3.9 0.0 copy-start.25
  3.9 0.6 copy-done.25
  4.5 0.1 broadcast_in_dim.5.refs_3_
  4.6 0.0 copy-done.1
  4.6 0.0 copy-done.2
  4.6 0.0 copy-done.3
  4.6 0.0 copy-done.4
  4.6 0.0 copy-done.5
  4.6 0.0 copy-done.6
  4.6 0.0 copy-done.7
  4.7 0.0 copy-done.8
  4.7 0.0 copy-done.9
  4.7 0.0 copy-done.10
  4.8 59.7 %shard_map.266 = (f32[256,256]{1,0:T(8,128)S(1)}, f32[8,128]{1,0:T(8,128)S(1)}) custom-call(f32[256,256]{1,0:T(8,128)S(1)} %copy-done.1, f32[256,256]{1,0:T(8,128)S(1)} %copy-done.2, f32[8,128]{1,0:T(8,128)S(1)} %broadcast_in_dim.4.refs_2_, f32[16,128]{1,0:T(8,128)S(1)} %broadcast_in_dim.5.refs_3_, f32[1024,128]{1,0:T(8,128)S(1)} %get-tuple-element.12.refs_4_, ...), custom_call_target="tpu_custom_call" | custom-call | tf_op jit(solution)/shard_map/pallas_call | solution.py:303
  64.5 0.5 slice_bitcast_fusion
  65.0 0.7 %copy.32 = f32[256,256]{1,0:T(8,128)} copy(f32[256,256]{1,0:T(8,128)S(1)} %get-tuple-element.16) | data formatting | bytes 524288
  (18 shorter events, 0.1 us)
Async XLA Ops:
  0.6 0.9 %copy-start = (f32[2,32,32]{2,1,0:T(8,128)S(1)}, f32[2,32,32]{2,1,0:T(8,128)}, u32[]{:S(2)}) copy-start(f32[2,32,32]{2,1,0:T(8,128)} %param.31) | copy-start | bytes 24580
  3.2 1.4 %copy-start.1 = (f32[256,256]{1,0:T(8,128)S(1)}, f32[256,256]{1,0:T(8,128)}, u32[]{:S(2)}) copy-start(f32[256,256]{1,0:T(8,128)} %refs_0_.1) | copy-start | bytes 786436
  3.2 1.4 %copy-start.2 = (f32[256,256]{1,0:T(8,128)S(1)}, f32[256,256]{1,0:T(8,128)}, u32[]{:S(2)}) copy-start(f32[256,256]{1,0:T(8,128)} %refs_1_.1) | copy-start | bytes 786436
  3.2 1.4 %copy-start.3 = (bf16[128,512]{1,0:T(8,128)(2,1)S(1)}, bf16[128,512]{1,0:T(8,128)(2,1)}, u32[]{:S(2)}) copy-start(bf16[128,512]{1,0:T(8,128)(2,1)} %constant.67.clone.refs_24_) | copy-start | bytes 393220
  3.2 1.4 %copy-start.4 = (bf16[128,512]{1,0:T(8,128)(2,1)S(1)}, bf16[128,512]{1,0:T(8,128)(2,1)}, u32[]{:S(2)}) copy-start(bf16[128,512]{1,0:T(8,128)(2,1)} %constant.68.clone.refs_25_) | copy-start | bytes 393220
  3.3 1.4 %copy-start.5 = (bf16[128,384]{1,0:T(8,128)(2,1)S(1)}, bf16[128,384]{1,0:T(8,128)(2,1)}, u32[]{:S(2)}) copy-start(bf16[128,384]{1,0:T(8,128)(2,1)} %constant.49.clone.refs_6_) | copy-start | bytes 294916
  3.3 1.4 %copy-start.6 = (bf16[128,384]{1,0:T(8,128)(2,1)S(1)}, bf16[128,384]{1,0:T(8,128)(2,1)}, u32[]{:S(2)}) copy-start(bf16[128,384]{1,0:T(8,128)(2,1)} %constant.50.clone.refs_7_) | copy-start | bytes 294916
  3.3 1.4 %copy-start.7 = (bf16[384,128]{1,0:T(8,128)(2,1)S(1)}, bf16[384,128]{1,0:T(8,128)(2,1)}, u32[]{:S(2)}) copy-start(bf16[384,128]{1,0:T(8,128)(2,1)} %constant.69.clone.refs_26_) | copy-start | bytes 294916
  3.3 1.4 %copy-start.8 = (bf16[384,128]{1,0:T(8,128)(2,1)S(1)}, bf16[384,128]{1,0:T(8,128)(2,1)}, u32[]{:S(2)}) copy-start(bf16[384,128]{1,0:T(8,128)(2,1)} %constant.70.clone.refs_27_) | copy-start | bytes 294916
  3.3 1.4 %copy-start.9 = (bf16[256,128]{1,0:T(8,128)(2,1)S(1)}, bf16[256,128]{1,0:T(8,128)(2,1)}, u32[]{:S(2)}) copy-start(bf16[256,128]{1,0:T(8,128)(2,1)} %constant.51.clone.refs_8_) | copy-start | bytes 196612
  3.3 1.4 %copy-start.10 = (bf16[256,128]{1,0:T(8,128)(2,1)S(1)}, bf16[256,128]{1,0:T(8,128)(2,1)}, u32[]{:S(2)}) copy-start(bf16[256,128]{1,0:T(8,128)(2,1)} %constant.52.clone.refs_9_) | copy-start | bytes 196612
  3.3 1.4 %copy-start.11 = (bf16[256,64]{1,0:T(8,128)(2,1)S(1)}, bf16[256,64]{1,0:T(8,128)(2,1)}, u32[]{:S(2)}) copy-start(bf16[256,64]{1,0:T(8,128)(2,1)} %constant.59.clone.refs_16_) | copy-start | bytes 98308
  3.3 1.4 %copy-start.12 = (bf16[256,64]{1,0:T(8,128)(2,1)S(1)}, bf16[256,64]{1,0:T(8,128)(2,1)}, u32[]{:S(2)}) copy-start(bf16[256,64]{1,0:T(8,128)(2,1)} %constant.60.clone.refs_17_) | copy-start | bytes 98308
  3.4 1.3 %copy-start.13 = (bf16[128,256]{1,0:T(8,128)(2,1)S(1)}, bf16[128,256]{1,0:T(8,128)(2,1)}, u32[]{:S(2)}) copy-start(bf16[128,256]{1,0:T(8,128)(2,1)} %constant.63.clone.refs_20_) | copy-start | bytes 196612
  3.4 1.3 %copy-start.14 = (bf16[128,256]{1,0:T(8,128)(2,1)S(1)}, bf16[128,256]{1,0:T(8,128)(2,1)}, u32[]{:S(2)}) copy-start(bf16[128,256]{1,0:T(8,128)(2,1)} %constant.64.clone.refs_21_) | copy-start | bytes 196612
  3.4 1.3 %copy-start.15 = (bf16[256,128]{1,0:T(8,128)(2,1)S(1)}, bf16[256,128]{1,0:T(8,128)(2,1)}, u32[]{:S(2)}) copy-start(bf16[256,128]{1,0:T(8,128)(2,1)} %constant.65.clone.refs_22_) | copy-start | bytes 196612
  3.4 1.3 %copy-start.16 = (bf16[256,128]{1,0:T(8,128)(2,1)S(1)}, bf16[256,128]{1,0:T(8,128)(2,1)}, u32[]{:S(2)}) copy-start(bf16[256,128]{1,0:T(8,128)(2,1)} %constant.66.clone.refs_23_) | copy-start | bytes 196612
  3.4 1.3 %copy-start.17 = (bf16[128,128]{1,0:T(8,128)(2,1)S(1)}, bf16[128,128]{1,0:T(8,128)(2,1)}, u32[]{:S(2)}) copy-start(bf16[128,128]{1,0:T(8,128)(2,1)} %constant.53.clone.refs_10_) | copy-start | bytes 98308
  3.4 1.3 %copy-start.18 = (bf16[128,128]{1,0:T(8,128)(2,1)S(1)}, bf16[128,128]{1,0:T(8,128)(2,1)}, u32[]{:S(2)}) copy-start(bf16[128,128]{1,0:T(8,128)(2,1)} %constant.54.clone.refs_11_) | copy-start | bytes 98308
  3.4 1.3 %copy-start.19 = (bf16[128,128]{1,0:T(8,128)(2,1)S(1)}, bf16[128,128]{1,0:T(8,128)(2,1)}, u32[]{:S(2)}) copy-start(bf16[128,128]{1,0:T(8,128)(2,1)} %constant.55.clone.refs_12_) | copy-start | bytes 98308
  3.4 1.3 %copy-start.20 = (bf16[128,128]{1,0:T(8,128)(2,1)S(1)}, bf16[128,128]{1,0:T(8,128)(2,1)}, u32[]{:S(2)}) copy-start(bf16[128,128]{1,0:T(8,128)(2,1)} %constant.56.clone.refs_13_) | copy-start | bytes 98308
  3.5 1.3 %copy-start.21 = (bf16[128,64]{1,0:T(8,128)(2,1)S(1)}, bf16[128,64]{1,0:T(8,128)(2,1)}, u32[]{:S(2)}) copy-start(bf16[128,64]{1,0:T(8,128)(2,1)} %constant.57.clone.refs_14_) | copy-start | bytes 49156
  3.5 1.3 %copy-start.22 = (bf16[128,64]{1,0:T(8,128)(2,1)S(1)}, bf16[128,64]{1,0:T(8,128)(2,1)}, u32[]{:S(2)}) copy-start(bf16[128,64]{1,0:T(8,128)(2,1)} %constant.58.clone.refs_15_) | copy-start | bytes 49156
  3.5 1.3 %copy-start.23 = (bf16[64,256]{1,0:T(8,128)(2,1)S(1)}, bf16[64,256]{1,0:T(8,128)(2,1)}, u32[]{:S(2)}) copy-start(bf16[64,256]{1,0:T(8,128)(2,1)} %constant.61.clone.refs_18_) | copy-start | bytes 98308
  3.5 1.3 %copy-start.24 = (bf16[64,256]{1,0:T(8,128)(2,1)S(1)}, bf16[64,256]{1,0:T(8,128)(2,1)}, u32[]{:S(2)}) copy-start(bf16[64,256]{1,0:T(8,128)(2,1)} %constant.62.clone.refs_19_) | copy-start | bytes 98308
  3.9 0.7 %copy-start.25 = (f32[16]{0:T(128)S(1)}, f32[16]{0:T(128)}, u32[]{:S(2)}) copy-start(f32[16]{0:T(128)} %param.29) | copy-start | bytes 196
where the time goes:
time: 65.9 us; the launch traced here: 65.7 us
  Pallas kernels  59.7 us (91%)
  local copies, waits for them, and re-layouts  2.98 us (5%)
  matrix products  1.56 us (2%)
  between operations  1.06 us (2%)
    pallas_call x1, Pallas kernels, per_device(): pl.pallas_call(functools.partial(kernel, ns, nt, 1.0 / (period * size)),...  59.7 us
    unnamed x53, local copies, waits for them, and re-layouts  1.53 us

commit v1 on v0

--- a/solution.py
+++ b/solution.py
@@ -41,7 +41,7 @@
     c, s = np.cos(g), np.sin(g)
     k1 = dirichlet(np.arange(tile) + MARGIN, period, box)
     k2 = dirichlet(np.arange(tile), period, box)
-    k2d = np.concatenate([k2.T, k2.T], 0)
+    k2d = np.concatenate([k2.T, np.zeros_like(k2.T)], 0)
     return dict(
         rf=np.concatenate([np.cos(row), np.sin(row)], 0),
         cf=np.concatenate([np.cos(col), np.sin(col)], 0).T,
@@ -51,12 +51,13 @@
         k1=k1,
         k1t=k1.T,
         k2d=k2d,
-        k2dt=k2d.T,
+        k2dt=np.concatenate([k2, k2], 1),
         col=np.block([[np.cos(col), np.sin(col)], [-np.sin(col), np.cos(col)]]),
         rfa=np.concatenate([np.cos(row), -np.sin(row)], 0).T,
     )
 
 
+LEFT = ("rf", "cs", "k1", "k1t", "rfa")
 NAMES = ("rf", "cf", "c2", "c2t", "cs", "k1", "k1t", "k2d", "k2dt", "col", "rfa")
 
 
@@ -67,6 +68,15 @@
     return high, low
 
 
+def packed(name, value):
+    high, low = split_np(value)
+    if name in ("c2", "c2t"):
+        return np.block([[high, low], [high, np.zeros_like(low)]])
+    if name in LEFT:
+        return np.concatenate([high, high, low], 1)
+    return np.concatenate([high, high, low], 0)
+
+
 def split(value):
     high = value.astype(bf16)
     return high, (value - high.astype(f32)).astype(bf16)
@@ -76,16 +86,27 @@
     return jnp.dot(a, b, preferred_element_type=f32)
 
 
-def dot3(a, b):
-    return dot(a[0], b[0]) + (dot(a[0], b[1]) + dot(a[1], b[0]))
+def left_dot(table, value):
+    high, low = split(value)
+    return dot(table, jnp.concatenate([high, low, high], 0))
+
+
+def right_dot(value, table):
+    high, low = split(value)
+    return dot(jnp.concatenate([high, low, high], 1), table)
+
+
+def wide_dot(value, table):
+    high, low = split(value)
+    both = dot(jnp.concatenate([high, low], 1), table)
+    width = value.shape[1]
+    return both[:, :width] + both[:, width:]
 
 
 def kernel(ns, nt, scale, *refs):
     mask_ref, target_ref, wl_ref, wb_ref, pa_ref, pb_ref = refs[:6]
-    consts = {
-        name: (refs[6 + 2 * i], refs[7 + 2 * i]) for i, name in enumerate(NAMES)
-    }
-    refs = refs[6 + 2 * len(NAMES):]
+    consts = {name: refs[6 + i] for i, name in enumerate(NAMES)}
+    refs = refs[6 + len(NAMES):]
     mask_out, weights_out = refs[:2]
     (params, grid, halo, dose_buf, power_buf, back_buf, next_buf, sq_buf, sg_buf, ss_buf,
      src_send, src_recv, tile_send, tile_recv) = refs[2:]
@@ -99,7 +120,7 @@
     half = width // 2
 
     def table(name):
-        return consts[name][0][...], consts[name][1][...]
+        return consts[name][...]
 
     def src_peer(r):
         return (group, lax.rem(src + r, ns), tile)
@@ -171,8 +192,7 @@
         return keep / (1.0 + jnp.exp(-params[...]))
 
     def imaging(mask, step):
-        first = dot3(table("rf"), split(mask))
-        quad = dot3(split(first), table("cf")) * scale
+        quad = right_dot(left_dot(table("rf"), mask), table("cf")) * scale
         spec = sign * quad[:half] - swap(quad[half:])
         spec_swap = swap(spec)
         parts = []
@@ -180,21 +200,27 @@
             rows = pl.ds(s * half, half)
             parts.append(pa_ref[rows] * spec + pb_ref[rows] * spec_swap)
         lit = jnp.concatenate(parts, 0)
-        mid = dot3(split(lit), table("c2"))
+        mid = wide_dot(lit, table("c2"))
         cs = table("cs")
         power = jnp.zeros((half, width), f32)
-        for s in range(count):
-            both = dot3(cs, split(mid[s * half:(s + 1) * half]))
-            z = both[:half] - sign * swap(both[half:])
-            grid[s] = z
-            power = power + wb_ref[s:s + 1] * (z * z)
+        for s in range(0, count, 2):
+            pair = [mid[i * half:(i + 1) * half] for i in range(s, s + 2)]
+            both = left_dot(cs, jnp.concatenate(pair, 1))
+            for i in range(2):
+                one = both[:, i * width:(i + 1) * width]
+                z = one[:half] - sign * swap(one[half:])
+                grid[s + i] = z
+                power = power + wb_ref[s + i:s + i + 1] * (z * z)
+        power = power + swap(power)
+        power = jnp.where(lane[:half // 2] < half, power[:half // 2], power[half // 2:])
         buf = power_buf.at[step]
         buf[src] = power
         landed(spread_src(buf))
         power = total(buf, ns)
-        bright = dot3(split(dot3(table("k1"), split(power))), table("k2d")) * inv_dose
+        power = jnp.concatenate([power, swap(power)], 0)
+        bright = right_dot(left_dot(table("k1"), power), table("k2d")) * inv_dose
         misfit = bright - target_ref[...]
-        pull = dot3(split(dot3(table("k1t"), split(misfit))), table("k2dt"))
+        pull = right_dot(left_dot(table("k1t"), misfit), table("k2dt"))
         return bright, misfit, pull
 
     for step in range(INNER_STEPS):
@@ -202,10 +228,13 @@
         bright, misfit, pull = imaging(mask, step)
         cs = table("cs")
         parts = []
-        for s in range(count):
-            both = dot3(cs, split(pull * grid[s]))
-            parts.append(both[:half] + sign * swap(both[half:]))
-        box = dot3(split(jnp.concatenate(parts, 0)), table("c2t"))
+        for s in range(0, count, 2):
+            pair = [pull * grid[i] for i in range(s, s + 2)]
+            both = left_dot(cs, jnp.concatenate(pair, 1))
+            for i in range(2):
+                part = both[:, i * width:(i + 1) * width]
+                parts.append(part[:half] + sign * swap(part[half:]))
+        box = wide_dot(jnp.concatenate(parts, 0), table("c2t"))
         one = jnp.zeros((half, width), f32)
         two = jnp.zeros((half, width), f32)
         for s in range(count):
@@ -224,16 +253,15 @@
         col = table("col")
 
         def values(spectrum):
-            wide = dot3(split(spectrum), col)
-            return split(jnp.concatenate([wide[:, :size], wide[:, size:]], 0))
-
-        grad = dot3(table("rfa"), values(back))
+            wide = right_dot(spectrum, col)
+            return jnp.concatenate([wide[:, :size], wide[:, size:]], 0)
+
+        grad = left_dot(table("rfa"), values(back))
         landed([to_next, to_prev])
         rim = 2 * MARGIN
-        high, low = consts["rfa"]
-        tail = pl.ds(period - rim, rim)
-        before = dot3((high[tail], low[tail]), values(own[0] * has_prev))
-        after = dot3((high[0:rim], low[0:rim]), values(own[1] * has_next))
+        rfa = consts["rfa"]
+        before = left_dot(rfa[pl.ds(period - rim, rim)], values(own[0] * has_prev))
+        after = left_dot(rfa[pl.ds(0, rim)], values(own[1] * has_next))
         grad = jnp.concatenate(
             [grad[:rim] + before, grad[rim:period - rim], grad[period - rim:] + after], 0
         )
@@ -259,8 +287,8 @@
     sums = (sums - level) * inv_dose
     lanes = lax.broadcasted_iota(jnp.int32, (count, 128), 1)
     ids = lax.broadcasted_iota(jnp.int32, (count, 128), 0)
-    packed = jnp.sum(jnp.where(lanes == ids, sums, 0.0), axis=0, keepdims=True)
-    sg_buf[tile] = jnp.broadcast_to(packed, (8, 128))
+    ordered = jnp.sum(jnp.where(lanes == ids, sums, 0.0), axis=0, keepdims=True)
+    sg_buf[tile] = jnp.broadcast_to(ordered, (8, 128))
     landed(spread_tile(sg_buf))
     slope = total(sg_buf, nt)
     ss_buf[src] = slope * slope
@@ -282,8 +310,7 @@
     consts = []
     made = tables(period, size, box)
     for name in NAMES:
-        high, low = split_np(made[name])
-        consts += [jnp.asarray(high), jnp.asarray(low)]
+        consts.append(jnp.asarray(packed(name, made[name])))
     highest = lax.Precision.HIGHEST
     base = jnp.arange(box, dtype=jnp.int32)[None, :, None] + MAX_SHIFT
     columns = jnp.arange(half, dtype=jnp.int32)[None, None, :]
@@ -313,7 +340,7 @@
             pltpu.VMEM((count, half, width), f32),
             pltpu.VMEM((2, MARGIN, size), f32),
             pltpu.VMEM((ns, 8, 128), f32),
-            pltpu.VMEM((INNER_STEPS + 1, ns, half, width), f32),
+            pltpu.VMEM((INNER_STEPS + 1, ns, half // 2, width), f32),
             pltpu.VMEM((INNER_STEPS, ns, half, width), f32),
             pltpu.VMEM((INNER_STEPS, 3, half, width), f32),
             pltpu.VMEM((INNER_STEPS, nt, 8, 128), f32),

time: 65.9 us -> 60.4 us (0.917)
  Pallas kernels: 59.7 us -> 54.1 us
    pallas_call x1, Pallas kernels: 59.7 us -> 54.1 us  [per_device(): pl.pallas_call(functools.partial(kernel, ns, nt, 1.0 / (period * size)),...]
    unnamed x53 -> x31, local copies, waits for them, and re-layouts: 1.53 us -> 1.82 us
where the time goes in v1:
time: 60.4 us; the launch traced here: 60.2 us
  Pallas kernels  54.1 us (90%)
  local copies, waits for them, and re-layouts  3.27 us (5%)
  matrix products  1.56 us (3%)
  between operations  0.86 us (1%)
    pallas_call x1, Pallas kernels, per_device(): pl.pallas_call(functools.partial(kernel, ns, nt, 1.0 / (period * size)),...  54.1 us
    unnamed x31, local copies, waits for them, and re-layouts  1.82 us

profile of v1, /device:TPU:0, one launch (start us, length us, event | category | flops | bytes accessed | tf_op | source)
XLA Modules:
  0.0 60.2 jit_solution(2505408624789356954)
XLA Ops:
  0.6 0.0 copy-start
  0.6 0.8 %slice_bitcast_fusion.1 = (s32[16]{0:T(128)S(1)}, s32[16]{0:T(128)S(1)}) fusion(s32[16,2]{0,1:T(2,128)} %param.19), kind=kLoop, calls=%fused_computation.14 | loop fusion | bytes 256 | tf_op jit(solution)/shard_map/slice | solution.py:318
  1.4 0.1 broadcast_add_fusion
  1.5 0.0 copy-done
  1.5 0.5 convolution_bitcast_fusion
  1.9 1.1 %fusion.3 = f32[16,2,64,64]{3,2,1,0:T(8,128)S(1)} fusion(f32[16,2,64,32]{2,3,1,0:T(8,128)S(1)} %convolution_bitcast_fusion, s32[16,32]{1,0:T(8,128)S(1)} %get-tuple-element.10), kind=kOutput, calls=%fused_computation.7 | convolution fusion | flops 50364416 | bytes 788480 | tf_op jit(solution)/shard_map/scjm,sml->scjl/dot_general | solution.py:320
  3.1 0.1 fusion.8
  3.2 0.0 copy-start.13
  3.2 0.0 copy-start.1
  3.2 0.0 copy-start.2
  3.2 0.0 copy-start.3
  3.3 0.0 copy-start.4
  3.3 0.0 copy-start.5
  3.3 0.0 copy-start.6
  3.3 0.0 copy-start.7
  3.3 0.0 copy-start.8
  3.3 0.0 copy-start.9
  3.3 0.0 copy-start.10
  3.3 0.0 copy-start.11
  3.4 0.0 copy-start.12
  3.4 0.3 pad_maximum_fusion
  3.7 0.0 copy-start.14
  3.7 0.9 %copy-done.14 = f32[16]{0:T(128)S(1)} copy-done((f32[16]{0:T(128)S(1)}, f32[16]{0:T(128)}, u32[]{:S(2)}) %copy-start.14) | copy-done | bytes 88
  4.6 0.1 broadcast_in_dim.5.refs_3_
  4.7 0.0 copy-done.13
  4.7 0.0 copy-done.1
  4.7 0.0 copy-done.2
  4.7 0.0 copy-done.3
  4.7 0.0 copy-done.4
  4.7 0.0 copy-done.5
  4.7 0.0 copy-done.6
  4.8 0.0 copy-done.7
  4.8 0.0 copy-done.8
  4.8 0.0 copy-done.9
  4.8 0.0 copy-done.10
  4.8 0.1 copy-done.11
  4.9 0.0 copy-done.12
  4.9 54.1 %shard_map.167 = (f32[256,256]{1,0:T(8,128)S(1)}, f32[8,128]{1,0:T(8,128)S(1)}) custom-call(f32[256,256]{1,0:T(8,128)S(1)} %copy-done.4, f32[256,256]{1,0:T(8,128)S(1)} %copy-done.5, f32[8,128]{1,0:T(8,128)S(1)} %broadcast_in_dim.4.refs_2_, f32[16,128]{1,0:T(8,128)S(1)} %broadcast_in_dim.5.refs_3_, f32[1024,128]{1,0:T(8,128)S(1)} %get-tuple-element.12.refs_4_, ...), custom_call_target="tpu_custom_call" | custom-call | tf_op jit(solution)/shard_map/pallas_call | solution.py:330
  59.0 0.5 slice_bitcast_fusion
  59.5 0.7 %copy.21 = f32[256,256]{1,0:T(8,128)} copy(f32[256,256]{1,0:T(8,128)S(1)} %get-tuple-element.16) | data formatting | bytes 524288
  (4 shorter events, 0.0 us)
Async XLA Ops:
  0.6 0.9 %copy-start = (f32[2,32,32]{2,1,0:T(8,128)S(1)}, f32[2,32,32]{2,1,0:T(8,128)}, u32[]{:S(2)}) copy-start(f32[2,32,32]{2,1,0:T(8,128)} %param.20) | copy-start | bytes 24580
  3.2 1.5 %copy-start.13 = (bf16[128,192]{1,0:T(8,128)(2,1)S(1)}, bf16[128,192]{1,0:T(8,128)(2,1)}, u32[]{:S(2)}) copy-start(bf16[128,192]{1,0:T(8,128)(2,1)} %constant.31.clone.refs_10_) | copy-start | bytes 147460
  3.2 1.5 %copy-start.1 = (bf16[384,512]{1,0:T(8,128)(2,1)S(1)}, bf16[384,512]{1,0:T(8,128)(2,1)}, u32[]{:S(2)}) copy-start(bf16[384,512]{1,0:T(8,128)(2,1)} %constant.36.clone.refs_15_) | copy-start | bytes 1179652
  3.2 1.5 %copy-start.2 = (bf16[128,1152]{1,0:T(8,128)(2,1)S(1)}, bf16[128,1152]{1,0:T(8,128)(2,1)}, u32[]{:S(2)}) copy-start(bf16[128,1152]{1,0:T(8,128)(2,1)} %constant.27.clone.refs_6_) | copy-start | bytes 884740
  3.2 1.5 %copy-start.3 = (bf16[384,384]{1,0:T(8,128)(2,1)S(1)}, bf16[384,384]{1,0:T(8,128)(2,1)}, u32[]{:S(2)}) copy-start(bf16[384,384]{1,0:T(8,128)(2,1)} %constant.37.clone.refs_16_) | copy-start | bytes 884740
  3.3 1.5 %copy-start.4 = (f32[256,256]{1,0:T(8,128)S(1)}, f32[256,256]{1,0:T(8,128)}, u32[]{:S(2)}) copy-start(f32[256,256]{1,0:T(8,128)} %refs_0_.1) | copy-start | bytes 786436
  3.3 1.5 %copy-start.5 = (f32[256,256]{1,0:T(8,128)S(1)}, f32[256,256]{1,0:T(8,128)}, u32[]{:S(2)}) copy-start(f32[256,256]{1,0:T(8,128)} %refs_1_.1) | copy-start | bytes 786436
  3.3 1.5 %copy-start.6 = (bf16[768,128]{1,0:T(8,128)(2,1)S(1)}, bf16[768,128]{1,0:T(8,128)(2,1)}, u32[]{:S(2)}) copy-start(bf16[768,128]{1,0:T(8,128)(2,1)} %constant.28.clone.refs_7_) | copy-start | bytes 589828
  3.3 1.5 %copy-start.7 = (bf16[384,256]{1,0:T(8,128)(2,1)S(1)}, bf16[384,256]{1,0:T(8,128)(2,1)}, u32[]{:S(2)}) copy-start(bf16[384,256]{1,0:T(8,128)(2,1)} %constant.34.clone.refs_13_) | copy-start | bytes 589828
  3.3 1.5 %copy-start.8 = (bf16[768,128]{1,0:T(8,128)(2,1)S(1)}, bf16[768,128]{1,0:T(8,128)(2,1)}, u32[]{:S(2)}) copy-start(bf16[768,128]{1,0:T(8,128)(2,1)} %constant.35.clone.refs_14_) | copy-start | bytes 589828
  3.3 1.5 %copy-start.9 = (bf16[256,256]{1,0:T(8,128)(2,1)S(1)}, bf16[256,256]{1,0:T(8,128)(2,1)}, u32[]{:S(2)}) copy-start(bf16[256,256]{1,0:T(8,128)(2,1)} %constant.29.clone.refs_8_) | copy-start | bytes 393220
  3.3 1.5 %copy-start.10 = (bf16[256,256]{1,0:T(8,128)(2,1)S(1)}, bf16[256,256]{1,0:T(8,128)(2,1)}, u32[]{:S(2)}) copy-start(bf16[256,256]{1,0:T(8,128)(2,1)} %constant.30.clone.refs_9_) | copy-start | bytes 393220
  3.3 1.5 %copy-start.11 = (bf16[256,192]{1,0:T(8,128)(2,1)S(1)}, bf16[256,192]{1,0:T(8,128)(2,1)}, u32[]{:S(2)}) copy-start(bf16[256,192]{1,0:T(8,128)(2,1)} %constant.32.clone.refs_11_) | copy-start | bytes 294916
  3.4 1.6 %copy-start.12 = (bf16[64,768]{1,0:T(8,128)(2,1)S(1)}, bf16[64,768]{1,0:T(8,128)(2,1)}, u32[]{:S(2)}) copy-start(bf16[64,768]{1,0:T(8,128)(2,1)} %constant.33.clone.refs_12_) | copy-start | bytes 294916
  3.7 0.9 %copy-start.14 = (f32[16]{0:T(128)S(1)}, f32[16]{0:T(128)}, u32[]{:S(2)}) copy-start(f32[16]{0:T(128)} %param.18) | copy-start | bytes 196

commit v2 on v1

--- a/solution.py
+++ b/solution.py
@@ -108,8 +108,8 @@
     consts = {name: refs[6 + i] for i, name in enumerate(NAMES)}
     refs = refs[6 + len(NAMES):]
     mask_out, weights_out = refs[:2]
-    (params, grid, halo, dose_buf, power_buf, back_buf, next_buf, sq_buf, sg_buf, ss_buf,
-     src_send, src_recv, tile_send, tile_recv) = refs[2:]
+    (params, grid, halo, dose_buf, power_buf, back_buf, next_buf, sq_buf, sg_buf,
+     src_send, src_recv, tile_send, tile_recv, all_send, all_recv) = refs[2:]
     group = lax.axis_index("group")
     src = lax.axis_index("src")
     tile = lax.axis_index("tile")
@@ -128,13 +128,19 @@
     def tile_peer(r):
         return (group, src, lax.rem(tile + r, nt))
 
+    everyone = [(a, b) for a in range(ns) for b in range(nt) if a or b]
+
+    def any_peer(a, b):
+        return (group, lax.rem(src + a, ns), lax.rem(tile + b, nt))
+
     pending = []
-    used = dict(src=0, tile=0)
+    used = dict(src=0, tile=0, all=0)
+    sems = dict(src=(src_send, src_recv), tile=(tile_send, tile_recv), all=(all_send, all_recv))
 
     def start(axis, source, target, peer):
         at = used[axis]
         used[axis] = at + 1
-        sends, recvs = (src_send, src_recv) if axis == "src" else (tile_send, tile_recv)
+        sends, recvs = sems[axis]
         copy = pltpu.make_async_remote_copy(
             src_ref=source, dst_ref=target, send_sem=sends.at[at], recv_sem=recvs.at[at],
             device_id=peer, device_id_type=MESH,
@@ -160,11 +166,9 @@
         return value
 
     barrier = pltpu.get_barrier_semaphore()
-    for r in range(1, ns):
-        pl.semaphore_signal(barrier, inc=1, device_id=src_peer(r), device_id_type=MESH)
-    for r in range(1, nt):
-        pl.semaphore_signal(barrier, inc=1, device_id=tile_peer(r), device_id_type=MESH)
-    pl.semaphore_wait(barrier, ns + nt - 2)
+    for a, b in everyone:
+        pl.semaphore_signal(barrier, inc=1, device_id=any_peer(a, b), device_id_type=MESH)
+    pl.semaphore_wait(barrier, ns * nt - 1)
 
     up = start("tile", mask_ref.at[pl.ds(size - MARGIN, MARGIN)], halo.at[0], tile_peer(1))
     down = start("tile", mask_ref.at[pl.ds(0, MARGIN)], halo.at[1], tile_peer(nt - 1))
@@ -174,9 +178,6 @@
     landed([up, down])
     params[pl.ds(0, MARGIN)] = halo[0]
     params[pl.ds(MARGIN + size, MARGIN)] = halo[1]
-    landed(dose_copies)
-    dose = jnp.sum(total(dose_buf, ns)[0:1], axis=1, keepdims=True)
-    inv_dose = 1.0 / dose
 
     has_prev = (tile > 0).astype(f32)
     has_next = (tile < nt - 1).astype(f32)
@@ -217,15 +218,19 @@
         buf[src] = power
         landed(spread_src(buf))
         power = total(buf, ns)
+        if step == 0:
+            landed(dose_copies)
+        dose = jnp.sum(total(dose_buf, ns)[0:1], axis=1, keepdims=True)
+        inv_dose = 1.0 / dose
         power = jnp.concatenate([power, swap(power)], 0)
         bright = right_dot(left_dot(table("k1"), power), table("k2d")) * inv_dose
         misfit = bright - target_ref[...]
         pull = right_dot(left_dot(table("k1t"), misfit), table("k2dt"))
-        return bright, misfit, pull
+        return bright, misfit, pull, inv_dose
 
     for step in range(INNER_STEPS):
         mask = sigmoid_mask()
-        bright, misfit, pull = imaging(mask, step)
+        bright, misfit, pull, inv_dose = imaging(mask, step)
         cs = table("cs")
         parts = []
         for s in range(0, count, 2):
@@ -277,7 +282,7 @@
         params[...] = params[...] - grad * (mask_rate / rms)
     mask_out[...] = params[pl.ds(MARGIN, size)]
 
-    bright, misfit, pull = imaging(sigmoid_mask(), INNER_STEPS)
+    bright, misfit, pull, inv_dose = imaging(sigmoid_mask(), INNER_STEPS)
     level = jnp.sum(misfit * bright, axis=0, keepdims=True)
     level = jnp.sum(level, axis=1, keepdims=True)
     rows = []
@@ -288,12 +293,19 @@
     lanes = lax.broadcasted_iota(jnp.int32, (count, 128), 1)
     ids = lax.broadcasted_iota(jnp.int32, (count, 128), 0)
     ordered = jnp.sum(jnp.where(lanes == ids, sums, 0.0), axis=0, keepdims=True)
-    sg_buf[tile] = jnp.broadcast_to(ordered, (8, 128))
-    landed(spread_tile(sg_buf))
-    slope = total(sg_buf, nt)
-    ss_buf[src] = slope * slope
-    landed(spread_src(ss_buf))
-    square = jnp.sum(total(ss_buf, ns)[0:1], axis=1, keepdims=True)
+    here = src * nt + tile
+    sg_buf[here] = jnp.broadcast_to(ordered, (8, 128))
+    landed([start("all", sg_buf.at[here], sg_buf.at[here], any_peer(a, b)) for a, b in everyone])
+    square = jnp.zeros((8, 128), f32)
+    for k in range(ns):
+        one = sg_buf[k * nt]
+        for i in range(1, nt):
+            one = one + sg_buf[k * nt + i]
+        square = square + one * one
+    slope = sg_buf[src * nt]
+    for i in range(1, nt):
+        slope = slope + sg_buf[src * nt + i]
+    square = jnp.sum(square[0:1], axis=1, keepdims=True)
     spread = jnp.sqrt(square / float(count * ns) + tiny_eps)
     weights_out[...] = wl_ref[...] * jnp.exp(-weight_rate * slope / spread)
     for copy in pending:
@@ -324,8 +336,8 @@
     wl = jnp.broadcast_to(jnp.pad(source_weights, (0, 128 - count))[None], (8, 128))
     wb = jnp.broadcast_to(source_weights[:, None], (count, width))
     vmem = pl.BlockSpec(memory_space=pltpu.VMEM)
-    src_sends = (ns - 1) * (2 + 2 * INNER_STEPS + 1)
-    tile_sends = 2 + INNER_STEPS * (2 + nt - 1) + (nt - 1)
+    src_sends = (ns - 1) * (2 + 2 * INNER_STEPS)
+    tile_sends = 2 + INNER_STEPS * (2 + nt - 1)
     args = (mask_param, target_image, wl, wb, pa, pb, *consts)
     mask_final, weights_final = pl.pallas_call(
         functools.partial(kernel, ns, nt, 1.0 / (period * size)),
@@ -344,12 +356,13 @@
             pltpu.VMEM((INNER_STEPS, ns, half, width), f32),
             pltpu.VMEM((INNER_STEPS, 3, half, width), f32),
             pltpu.VMEM((INNER_STEPS, nt, 8, 128), f32),
-            pltpu.VMEM((nt, 8, 128), f32),
-            pltpu.VMEM((ns, 8, 128), f32),
+            pltpu.VMEM((ns * nt, 8, 128), f32),
             pltpu.SemaphoreType.DMA((src_sends,)),
             pltpu.SemaphoreType.DMA((src_sends,)),
             pltpu.SemaphoreType.DMA((tile_sends,)),
             pltpu.SemaphoreType.DMA((tile_sends,)),
+            pltpu.SemaphoreType.DMA((ns * nt - 1,)),
+            pltpu.SemaphoreType.DMA((ns * nt - 1,)),
         ],
         compiler_params=pltpu.CompilerParams(
             collective_id=0, has_side_effects=True, vmem_limit_bytes=48 * 1024 * 1024

time: 60.4 us -> 59 us (0.977)
  Pallas kernels: 54.1 us -> 52.7 us
    pallas_call x1, Pallas kernels: 54.1 us -> 52.7 us  [per_device(): pl.pallas_call(functools.partial(kernel, ns, nt, 1.0 / (period * size)),...]
where the time goes in v2:
time: 59 us; the launch traced here: 58.8 us
  Pallas kernels  52.7 us (89%)
  local copies, waits for them, and re-layouts  3.27 us (6%)
  matrix products  1.56 us (3%)
  between operations  0.86 us (1%)
    pallas_call x1, Pallas kernels, per_device(): pl.pallas_call(functools.partial(kernel, ns, nt, 1.0 / (period * size)),...  52.7 us
    unnamed x31, local copies, waits for them, and re-layouts  1.82 us

profile of v2, /device:TPU:0, one launch (start us, length us, event | category | flops | bytes accessed | tf_op | source)
XLA Modules:
  0.0 58.8 jit_solution(11639566165613042876)
XLA Ops:
  0.6 0.0 copy-start
  0.6 0.8 %slice_bitcast_fusion.1 = (s32[16]{0:T(128)S(1)}, s32[16]{0:T(128)S(1)}) fusion(s32[16,2]{0,1:T(2,128)} %param.19), kind=kLoop, calls=%fused_computation.14 | loop fusion | bytes 256 | tf_op jit(solution)/shard_map/slice | solution.py:330
  1.4 0.1 broadcast_add_fusion
  1.5 0.0 copy-done
  1.5 0.5 convolution_bitcast_fusion
  1.9 1.1 %fusion.3 = f32[16,2,64,64]{3,2,1,0:T(8,128)S(1)} fusion(f32[16,2,64,32]{2,3,1,0:T(8,128)S(1)} %convolution_bitcast_fusion, s32[16,32]{1,0:T(8,128)S(1)} %get-tuple-element.10), kind=kOutput, calls=%fused_computation.7 | convolution fusion | flops 50364416 | bytes 788480 | tf_op jit(solution)/shard_map/scjm,sml->scjl/dot_general | solution.py:332
  3.1 0.1 fusion.8
  3.2 0.0 copy-start.13
  3.2 0.0 copy-start.1
  3.2 0.0 copy-start.2
  3.2 0.0 copy-start.3
  3.3 0.0 copy-start.4
  3.3 0.0 copy-start.5
  3.3 0.0 copy-start.6
  3.3 0.0 copy-start.7
  3.3 0.0 copy-start.8
  3.3 0.0 copy-start.9
  3.3 0.0 copy-start.10
  3.3 0.0 copy-start.11
  3.4 0.0 copy-start.12
  3.4 0.3 pad_maximum_fusion
  3.7 0.0 copy-start.14
  3.7 0.9 %copy-done.14 = f32[16]{0:T(128)S(1)} copy-done((f32[16]{0:T(128)S(1)}, f32[16]{0:T(128)}, u32[]{:S(2)}) %copy-start.14) | copy-done | bytes 88
  4.6 0.1 broadcast_in_dim.5.refs_3_
  4.7 0.0 copy-done.13
  4.7 0.0 copy-done.1
  4.7 0.0 copy-done.2
  4.7 0.0 copy-done.3
  4.7 0.0 copy-done.4
  4.7 0.0 copy-done.5
  4.7 0.0 copy-done.6
  4.8 0.0 copy-done.7
  4.8 0.0 copy-done.8
  4.8 0.0 copy-done.9
  4.8 0.0 copy-done.10
  4.8 0.1 copy-done.11
  4.9 0.0 copy-done.12
  4.9 52.7 %shard_map.167 = (f32[256,256]{1,0:T(8,128)S(1)}, f32[8,128]{1,0:T(8,128)S(1)}) custom-call(f32[256,256]{1,0:T(8,128)S(1)} %copy-done.4, f32[256,256]{1,0:T(8,128)S(1)} %copy-done.5, f32[8,128]{1,0:T(8,128)S(1)} %broadcast_in_dim.4.refs_2_, f32[16,128]{1,0:T(8,128)S(1)} %broadcast_in_dim.5.refs_3_, f32[1024,128]{1,0:T(8,128)S(1)} %get-tuple-element.12.refs_4_, ...), custom_call_target="tpu_custom_call" | custom-call | tf_op jit(solution)/shard_map/pallas_call | solution.py:342
  57.6 0.5 slice_bitcast_fusion
  58.1 0.7 %copy.21 = f32[256,256]{1,0:T(8,128)} copy(f32[256,256]{1,0:T(8,128)S(1)} %get-tuple-element.16) | data formatting | bytes 524288
  (4 shorter events, 0.0 us)
Async XLA Ops:
  0.6 0.9 %copy-start = (f32[2,32,32]{2,1,0:T(8,128)S(1)}, f32[2,32,32]{2,1,0:T(8,128)}, u32[]{:S(2)}) copy-start(f32[2,32,32]{2,1,0:T(8,128)} %param.20) | copy-start | bytes 24580
  3.2 1.5 %copy-start.13 = (bf16[128,192]{1,0:T(8,128)(2,1)S(1)}, bf16[128,192]{1,0:T(8,128)(2,1)}, u32[]{:S(2)}) copy-start(bf16[128,192]{1,0:T(8,128)(2,1)} %constant.31.clone.refs_10_) | copy-start | bytes 147460
  3.2 1.5 %copy-start.1 = (bf16[384,512]{1,0:T(8,128)(2,1)S(1)}, bf16[384,512]{1,0:T(8,128)(2,1)}, u32[]{:S(2)}) copy-start(bf16[384,512]{1,0:T(8,128)(2,1)} %constant.36.clone.refs_15_) | copy-start | bytes 1179652
  3.2 1.5 %copy-start.2 = (bf16[128,1152]{1,0:T(8,128)(2,1)S(1)}, bf16[128,1152]{1,0:T(8,128)(2,1)}, u32[]{:S(2)}) copy-start(bf16[128,1152]{1,0:T(8,128)(2,1)} %constant.27.clone.refs_6_) | copy-start | bytes 884740
  3.2 1.5 %copy-start.3 = (bf16[384,384]{1,0:T(8,128)(2,1)S(1)}, bf16[384,384]{1,0:T(8,128)(2,1)}, u32[]{:S(2)}) copy-start(bf16[384,384]{1,0:T(8,128)(2,1)} %constant.37.clone.refs_16_) | copy-start | bytes 884740
  3.3 1.5 %copy-start.4 = (f32[256,256]{1,0:T(8,128)S(1)}, f32[256,256]{1,0:T(8,128)}, u32[]{:S(2)}) copy-start(f32[256,256]{1,0:T(8,128)} %refs_0_.1) | copy-start | bytes 786436
  3.3 1.5 %copy-start.5 = (f32[256,256]{1,0:T(8,128)S(1)}, f32[256,256]{1,0:T(8,128)}, u32[]{:S(2)}) copy-start(f32[256,256]{1,0:T(8,128)} %refs_1_.1) | copy-start | bytes 786436
  3.3 1.5 %copy-start.6 = (bf16[768,128]{1,0:T(8,128)(2,1)S(1)}, bf16[768,128]{1,0:T(8,128)(2,1)}, u32[]{:S(2)}) copy-start(bf16[768,128]{1,0:T(8,128)(2,1)} %constant.28.clone.refs_7_) | copy-start | bytes 589828
  3.3 1.5 %copy-start.7 = (bf16[384,256]{1,0:T(8,128)(2,1)S(1)}, bf16[384,256]{1,0:T(8,128)(2,1)}, u32[]{:S(2)}) copy-start(bf16[384,256]{1,0:T(8,128)(2,1)} %constant.34.clone.refs_13_) | copy-start | bytes 589828
  3.3 1.5 %copy-start.8 = (bf16[768,128]{1,0:T(8,128)(2,1)S(1)}, bf16[768,128]{1,0:T(8,128)(2,1)}, u32[]{:S(2)}) copy-start(bf16[768,128]{1,0:T(8,128)(2,1)} %constant.35.clone.refs_14_) | copy-start | bytes 589828
  3.3 1.5 %copy-start.9 = (bf16[256,256]{1,0:T(8,128)(2,1)S(1)}, bf16[256,256]{1,0:T(8,128)(2,1)}, u32[]{:S(2)}) copy-start(bf16[256,256]{1,0:T(8,128)(2,1)} %constant.29.clone.refs_8_) | copy-start | bytes 393220
  3.3 1.5 %copy-start.10 = (bf16[256,256]{1,0:T(8,128)(2,1)S(1)}, bf16[256,256]{1,0:T(8,128)(2,1)}, u32[]{:S(2)}) copy-start(bf16[256,256]{1,0:T(8,128)(2,1)} %constant.30.clone.refs_9_) | copy-start | bytes 393220
  3.3 1.5 %copy-start.11 = (bf16[256,192]{1,0:T(8,128)(2,1)S(1)}, bf16[256,192]{1,0:T(8,128)(2,1)}, u32[]{:S(2)}) copy-start(bf16[256,192]{1,0:T(8,128)(2,1)} %constant.32.clone.refs_11_) | copy-start | bytes 294916
  3.4 1.6 %copy-start.12 = (bf16[64,768]{1,0:T(8,128)(2,1)S(1)}, bf16[64,768]{1,0:T(8,128)(2,1)}, u32[]{:S(2)}) copy-start(bf16[64,768]{1,0:T(8,128)(2,1)} %constant.33.clone.refs_12_) | copy-start | bytes 294916
  3.7 0.9 %copy-start.14 = (f32[16]{0:T(128)S(1)}, f32[16]{0:T(128)}, u32[]{:S(2)}) copy-start(f32[16]{0:T(128)} %param.18) | copy-start | bytes 196
